TPU v7x, 512 devices: a whole 4x4x16 slice. The times are simulated.
512 devices in a mesh: grp: 16 (over y, z_hi), par: 32 (over z_lo, x, core).
Axes of the slice: x: 4, y: 4, z: 16 (z_hi: 4, z_lo: 4; z = z_hi * 4 + z_lo), core: 2. Of those that a mesh axis runs over, the one named last changes fastest.
Arguments:
- particles: float32 [64, 1048576], P('grp', 'par'), may hold values from -6 to 6
- scores: float32 [64, 1048576], P('grp', 'par'), may hold values from -6 to 6
- kernel_width: float32 [1], replicated, may hold values from 1 to 4
Outputs:
- drive: float32 [64, 1048576], P('grp', 'par')
- repel: float32 [64, 1048576], P('grp', 'par')
All inputs are finite; a program needn't handle non-finite values.
Results may differ from a plain program's by a relative error of at most 0.000092.
Values sent between devices are 32-bit elements; how exact they have to be, the bound alone decides.
A program may use at most 128 MiB of HBM per device.

v0:
```python
import jax
import jax.numpy as jnp
from jax import lax
from jax.sharding import PartitionSpec as P

P_SIZE = 1048576


def cross(left, right):
    return lax.dot_general(
        left,
        right,
        (((1,), (1,)), ((), ())),
        precision=lax.Precision.HIGHEST,
        preferred_element_type=jnp.float32,
    )


def weigh(kern, block):
    return jnp.dot(kern, block, precision=lax.Precision.HIGHEST, preferred_element_type=jnp.float32)


def shards(particles, scores, kernel_width):
    scale = kernel_width[0] * P_SIZE
    groups = lax.axis_size("grp")
    count = particles.shape[0] * groups
    own_norm = jnp.sum(particles * particles, axis=1)
    every_x, every_s = (
        lax.all_gather(particles, "grp", axis=0, tiled=True),
        lax.all_gather(scores, "grp", axis=0, tiled=True),
    )
    every_norm = jnp.sum(every_x * every_x, axis=1)
    partial_dist = own_norm[:, None] + every_norm[None, :] - 2.0 * cross(particles, every_x)
    dist = lax.psum(partial_dist, "par")
    kern = jnp.exp(-dist / scale)
    drive_sum = weigh(kern, every_s)
    pull = weigh(kern, every_x)
    weight = jnp.sum(kern, axis=1)
    drive = drive_sum / count
    repel = (particles * weight[:, None] - pull) / (count * kernel_width[0])
    return (drive, repel)


def solution(mesh):
    return jax.shard_map(
        shards,
        mesh=mesh,
        in_specs=(P("grp", "par"), P("grp", "par"), P()),
        out_specs=(P("grp", "par"), P("grp", "par")),
        check_vma=False,
    )
```

profile of v0, /device:TPU:1, one launch (start us, length us, event | category | flops | bytes accessed | tf_op | source)
XLA Modules:
  0.0 479.5 jit_solution(1377976601495616386)
XLA Ops:
  7.2 0.0 all-gather.5.cloned.1.call-start
  7.2 0.7 all-gather.5.cloned.1.call-update
  7.9 0.0 all-gather.7.cloned.1.call-start
  7.9 0.7 all-gather.7.cloned.1.call-update
  9.3 1.4 multiply_reduce_fusion.1
  10.7 221.4 %all-gather.5.cloned.1.call-done = f32[16,4,32768]{2,1,0:T(4,128)} async-done(((f32[1,4,32768]{2,1,0:T(4,128)}), f32[16,4,32768]{2,1,0:T(4,128)}) %all-gather.5.cloned.1.call-update) | async-done | bytes 8388624 | tf_op jit(solution)/shard_map/all_gather | solution.py:29
  232.1 0.0 copy-start.1
  232.1 10.0 %reshape.12 = f32[64,32768]{1,0:T(8,128)} reshape(f32[16,4,32768]{2,1,0:T(4,128)} %all-gather.5.cloned.1.call-done) | data formatting | bytes 16777216
  242.2 0.0 copy-start
  242.2 4.2 multiply_reduce_fusion
  246.4 0.0 copy-done.1
  246.4 1.6 copy-done
  247.9 6.6 %fusion.1 = f32[4,64]{1,0:T(4,128)S(1)} fusion(f32[4,32768]{1,0:T(4,128)S(1)} %copy-done.1, f32[64,32768]{1,0:T(8,128)S(1)} %copy-done, f32[64]{0:T(128)S(1)} %multiply_reduce_fusion, f32[4]{0:T(128)S(1)} %multiply_reduce_fusion.1), kind=kOutput, calls=%fused_computation.5 | convolution fusion | flops 100664064 | bytes 8914192 | tf_op jit(solution)/shard_map/dot_general | solution.py:10
  254.5 84.9 %psum.7 = f32[4,64]{1,0:T(4,128)S(1)} all-reduce(f32[4,64]{1,0:T(4,128)S(1)} %fusion.1), channel_id=1, replica_groups=mesh['grp'=16,'par'=32] {'par'}, use_global_device_ids=true, to_apply=%region_2.0 | all-reduce | flops 256 | bytes 2048 | tf_op jit(solution)/shard_map/psum | solution.py:34
  339.4 0.1 fusion.2
  339.5 109.1 %all-gather.7.cloned.1.call-done = f32[16,4,32768]{2,1,0:T(4,128)} async-done(((f32[1,4,32768]{2,1,0:T(4,128)}), f32[16,4,32768]{2,1,0:T(4,128)}) %all-gather.7.cloned.1.call-update) | async-done | bytes 8388624 | tf_op jit(solution)/shard_map/all_gather | solution.py:30
  448.6 10.0 %reshape.14 = f32[64,32768]{1,0:T(8,128)} reshape(f32[16,4,32768]{2,1,0:T(4,128)} %all-gather.7.cloned.1.call-done) | data formatting | bytes 16777216
  458.6 7.1 %convolution_multiply_fusion = f32[4,32768]{1,0:T(4,128)} fusion(f32[64,32768]{1,0:T(8,128)} %reshape.14, f32[4,64]{1,0:T(4,128)S(1)} %psum.7, f32[]{:T(128)} %bitcast.1), kind=kOutput, calls=%fused_computation.2 | convolution fusion | flops 100794880 | bytes 8913924 | tf_op jit(solution)/shard_map/dot_general | solution.py:20
  465.6 7.1 %fusion = f32[4,32768]{1,0:T(4,128)} fusion(f32[64,32768]{1,0:T(8,128)} %reshape.12, f32[4,32768]{1,0:T(4,128)S(1)} %copy-done.1, f32[]{:T(128)} %bitcast.3, f32[4]{0:T(128)S(1)} %fusion.2, f32[4,64]{1,0:T(4,128)S(1)} %psum.7, f32[]{:T(128)} %bitcast.1), kind=kOutput, calls=%fused_computation.1 | convolution fusion | flops 101057024 | bytes 9438232 | tf_op jit(solution)/shard_map/dot_general | solution.py:20
Async XLA Ops:
  7.2 225.0 %all-gather.5.cloned.1.call-start = ((), (), s32[]{:S(2)}) async-start(), calls=%async_computation | async-start | bytes 8912896 | tf_op jit(solution)/shard_map/all_gather | solution.py:29
  7.9 440.7 %all-gather.7.cloned.1.call-start = ((), (), s32[]{:S(2)}) async-start(), calls=%async_computation.1 | async-start | bytes 8912896 | tf_op jit(solution)/shard_map/all_gather | solution.py:30
  232.1 14.2 %copy-start.1 = (f32[4,32768]{1,0:T(4,128)S(1)}, f32[4,32768]{1,0:T(4,128)}, u32[]{:S(2)}) copy-start(f32[4,32768]{1,0:T(4,128)} %param.3) | copy-start | bytes 1572868
  242.2 5.8 %copy-start = (f32[64,32768]{1,0:T(8,128)S(1)}, f32[64,32768]{1,0:T(8,128)}, u32[]{:S(2)}) copy-start(f32[64,32768]{1,0:T(8,128)} %reshape.12) | copy-start | bytes 25165828
Sparse Core Ops, SparseCore 0:
  11.0 221.0 all-gather.4
  235.2 213.4 all-gather.6
where the time goes:
time: 481 us; the launch traced here: 480 us
  waiting for transfers between devices  332 us (69%)
  blocking collectives  84.9 us (18%)
  local copies, waits for them, and re-layouts  21.6 us (4%)
  matrix products  20.7 us (4%)
  between operations  14.7 us (3%)
  other arithmetic  5.72 us (1%)
    all_gather x1, waiting for transfers between devices, shards(): lax.all_gather(particles, 'grp', axis=0, tiled=True)  221 us
    all_gather x1, waiting for transfers between devices, shards(): lax.all_gather(scores, 'grp', axis=0, tiled=True)  109 us
    psum x1, blocking collectives, shards(): dist = lax.psum(partial_dist, 'par')  84.9 us
    unnamed x6, local copies, waits for them, and re-layouts  21.6 us
    dot_general x2, matrix products, weigh(): jnp.dot(kern, block, precision=lax.Precision.HIGHEST, preferred_element_t...  14.1 us
  transfers between devices with their start and end apart: 2, of which 2 were waited for; matrix products, arithmetic and copies ran while one was open for 5% of the time, Pallas kernels for 0%

commit v1 on v0

v1 whole, which is shorter than its diff:
```python
import jax
import jax.numpy as jnp
from jax import lax
from jax.sharding import PartitionSpec as P

P_SIZE = 1048576
HIGHEST = lax.Precision.HIGHEST


def shards(particles, scores, kernel_width):
    width = kernel_width[0]
    groups = lax.axis_size("grp")
    count = particles.shape[0] * groups
    x = lax.all_to_all(particles, "grp", split_axis=1, concat_axis=0, tiled=True)
    s = lax.all_to_all(scores, "grp", split_axis=1, concat_axis=0, tiled=True)
    norms = jnp.sum(x * x, axis=1)
    inner = lax.dot_general(x, x, (((1,), (1,)), ((), ())), precision=HIGHEST, preferred_element_type=jnp.float32)
    dist = lax.psum(norms[:, None] + norms[None, :] - 2.0 * inner, ("grp", "par"))
    kern = jnp.exp(-dist / (width * P_SIZE))
    drive = jnp.dot(kern, s, precision=HIGHEST) / count
    pull = jnp.dot(kern, x, precision=HIGHEST)
    weight = jnp.sum(kern, axis=1)
    repel = (x * weight[:, None] - pull) / (count * width)
    drive = lax.all_to_all(drive, "grp", split_axis=0, concat_axis=1, tiled=True)
    repel = lax.all_to_all(repel, "grp", split_axis=0, concat_axis=1, tiled=True)
    return (drive, repel)


def solution(mesh):
    return jax.shard_map(
        shards,
        mesh=mesh,
        in_specs=(P("grp", "par"), P("grp", "par"), P()),
        out_specs=(P("grp", "par"), P("grp", "par")),
        check_vma=False,
    )
```

time: 481 us -> 245 us (0.51)
  waiting for transfers between devices: 332 us -> 57 us
  blocking collectives: 84.9 us -> 154 us
  starting transfers between devices: 0.08 us -> 25.1 us
  matrix products: 20.7 us -> 1.74 us
  local copies, waits for them, and re-layouts: 21.6 us -> 3.92 us
  between operations: 14.7 us -> 1.35 us
  other arithmetic: 5.72 us -> 0.3 us
    all_gather x2 -> x0, waiting for transfers between devices: 330 us -> none  [the longest x1 221 us: shards(): lax.all_gather(particles, 'grp', axis=0, tiled=True)]
    all_to_all x0 -> x3, waiting for transfers between devices: none -> 57 us  [the longest x1 29.6 us: shards(): lax.all_to_all(drive, 'grp', split_axis=0, concat_axis=1, tiled=True)]
    all_to_all x0 -> x1, blocking collectives: none -> 45.6 us  [shards(): lax.all_to_all(particles, 'grp', split_axis=1, concat_axis=0, tiled=True)]
    all_to_all x0 -> x3, starting transfers between devices: none -> 25.1 us  [the longest x1 8.59 us: shards(): lax.all_to_all(repel, 'grp', split_axis=0, concat_axis=1, tiled=True)]
    psum x1, blocking collectives: 84.9 us -> 108 us  [shards(): lax.psum(norms[:, None] + norms[None, :] - 2.0 * inner, ('grp', 'par'))]
    unnamed x6 -> x2, local copies, waits for them, and re-layouts: 21.6 us -> 1.59 us
    dot_general x3, matrix products: 20.7 us -> 1.74 us  [the longest x1 0.6 us: shards(): pull = jnp.dot(kern, x, precision=HIGHEST)]
    reduce_sum x2 -> x1, other arithmetic: 5.6 us -> 0.18 us  [shards(): norms = jnp.sum(x * x, axis=1)]
  transfers between devices with their start and end apart: 2 -> 3, of which waited for: 2 -> 2; matrix products, arithmetic and copies ran while one was open for 5% -> 1% of each run, Pallas kernels for 0% -> 0%
where the time goes in v1:
time: 245 us; the launch traced here: 243 us
  blocking collectives  154 us (63%)
  waiting for transfers between devices  57 us (23%)
  starting transfers between devices  25.1 us (10%)
  local copies, waits for them, and re-layouts  3.92 us (2%)
    psum x1, blocking collectives, shards(): lax.psum(norms[:, None] + norms[None, :] - 2.0 * inner, ('grp', 'par'))  108 us
    all_to_all x1, blocking collectives, shards(): lax.all_to_all(particles, 'grp', split_axis=1, concat_axis=0, tiled=True)  45.6 us
    all_to_all x1, waiting for transfers between devices, shards(): lax.all_to_all(drive, 'grp', split_axis=0, concat_axis=1, tiled=True)  29.6 us
    all_to_all x1, waiting for transfers between devices, shards(): lax.all_to_all(repel, 'grp', split_axis=0, concat_axis=1, tiled=True)  27.4 us
    all_to_all x1, starting transfers between devices, shards(): lax.all_to_all(repel, 'grp', split_axis=0, concat_axis=1, tiled=True)  8.59 us
    all_to_all x1, starting transfers between devices, shards(): s = lax.all_to_all(scores, 'grp', split_axis=1, concat_axis=0, tiled=True)  8.5 us
    all_to_all x1, starting transfers between devices, shards(): lax.all_to_all(drive, 'grp', split_axis=0, concat_axis=1, tiled=True)  7.98 us
  transfers between devices with their start and end apart: 3, of which 2 were waited for; matrix products, arithmetic and copies ran while one was open for 1% of the time, Pallas kernels for 0%

profile of v1, /device:TPU:1, one launch (start us, length us, event | category | flops | bytes accessed | tf_op | source)
XLA Modules:
  0.0 243.1 jit_solution(5901329708287473420)
XLA Ops:
  0.6 45.6 %all_to_all.76 = f32[4,16,2048]{2,0,1:T(4,128)S(1)} all-to-all(f32[4,16,2048]{2,0,1:T(4,128)} %bitcast.21), channel_id=1, replica_groups=mesh['grp'=16,'par'=32] {'grp'}, dimensions={1} | all-to-all | bytes 1048576 | tf_op jit(solution)/shard_map/all_to_all | solution.py:14
  46.2 8.5 %all-to-all-start.1 = ((f32[4,16,2048]{2,0,1:T(4,128)}), f32[4,16,2048]{2,0,1:T(4,128)S(1)}, u32[]{:S(2)}, u32[]{:S(2)}) async-start(f32[4,16,2048]{2,0,1:T(4,128)} %bitcast.3), calls=%async_computation.1 | async-start | bytes 1048576 | tf_op jit(solution)/shard_map/all_to_all | solution.py:15
  55.3 0.2 all_to_all.59
  55.5 0.2 multiply_reduce_fusion
  55.7 0.1 add.17
  55.8 0.6 fusion.1
  56.4 108.2 %psum.7 = f32[64,64]{1,0:T(8,128)S(1)} all-reduce(f32[64,64]{1,0:T(8,128)S(1)} %fusion.1), channel_id=1, replica_groups=mesh['grp'=16,'par'=32] {'grp','par'}, use_global_device_ids=true, to_apply=%region_1.0 | all-reduce | flops 4096 | bytes 32768 | tf_op jit(solution)/shard_map/psum | solution.py:18
  164.5 0.1 fusion.2
  164.7 0.6 fusion
  165.3 0.9 all_to_all.68
  166.2 0.0 all-to-all-done.1
  166.2 8.6 %all-to-all-start.3 = ((f32[16,4,2048]{2,1,0:T(4,128)}), f32[16,4,2048]{2,1,0:T(4,128)S(1)}, u32[]{:S(2)}, u32[]{:S(2)}) async-start(f32[16,4,2048]{2,1,0:T(4,128)} %all_to_all.68), calls=%async_computation.3 | async-start | bytes 1048576 | tf_op jit(solution)/shard_map/all_to_all | solution.py:25
  174.8 0.2 all_to_all.63
  175.0 0.6 convolution_multiply_fusion
  175.6 0.9 all_to_all.64
  176.5 27.4 %all-to-all-done.3 = f32[16,4,2048]{2,1,0:T(4,128)S(1)} async-done(((f32[16,4,2048]{2,1,0:T(4,128)}), f32[16,4,2048]{2,1,0:T(4,128)S(1)}, u32[]{:S(2)}, u32[]{:S(2)}) %all-to-all-start.3) | async-done | bytes 524320 | tf_op jit(solution)/shard_map/all_to_all | solution.py:25
  203.9 8.0 %all-to-all-start.2 = ((f32[16,4,2048]{2,1,0:T(4,128)}), f32[16,4,2048]{2,1,0:T(4,128)S(1)}, u32[]{:S(2)}, u32[]{:S(2)}) async-start(f32[16,4,2048]{2,1,0:T(4,128)} %all_to_all.64), calls=%async_computation.2 | async-start | bytes 1048576 | tf_op jit(solution)/shard_map/all_to_all | solution.py:24
  211.9 29.6 %all-to-all-done.2 = f32[16,4,2048]{2,1,0:T(4,128)S(1)} async-done(((f32[16,4,2048]{2,1,0:T(4,128)}), f32[16,4,2048]{2,1,0:T(4,128)S(1)}, u32[]{:S(2)}, u32[]{:S(2)}) %all-to-all-start.2) | async-done | bytes 524320 | tf_op jit(solution)/shard_map/all_to_all | solution.py:24
  241.5 0.8 copy.15
  242.3 0.8 copy.16
Async XLA Ops:
  46.2 120.0 %all-to-all-start.1 = ((f32[4,16,2048]{2,0,1:T(4,128)}), f32[4,16,2048]{2,0,1:T(4,128)S(1)}, u32[]{:S(2)}, u32[]{:S(2)}) async-start(f32[4,16,2048]{2,0,1:T(4,128)} %bitcast.3), calls=%async_computation.1 | async-start | bytes 1048576 | tf_op jit(solution)/shard_map/all_to_all | solution.py:15
  166.2 37.7 %all-to-all-start.3 = ((f32[16,4,2048]{2,1,0:T(4,128)}), f32[16,4,2048]{2,1,0:T(4,128)S(1)}, u32[]{:S(2)}, u32[]{:S(2)}) async-start(f32[16,4,2048]{2,1,0:T(4,128)} %all_to_all.68), calls=%async_computation.3 | async-start | bytes 1048576 | tf_op jit(solution)/shard_map/all_to_all | solution.py:25
  203.9 37.6 %all-to-all-start.2 = ((f32[16,4,2048]{2,1,0:T(4,128)}), f32[16,4,2048]{2,1,0:T(4,128)S(1)}, u32[]{:S(2)}, u32[]{:S(2)}) async-start(f32[16,4,2048]{2,1,0:T(4,128)} %all_to_all.64), calls=%async_computation.2 | async-start | bytes 1048576 | tf_op jit(solution)/shard_map/all_to_all | solution.py:24

commit v2 on v1

v2 whole, which is shorter than its diff:
```python
import jax
import jax.numpy as jnp
from jax import lax
from jax.experimental import pallas as pl
from jax.experimental.pallas import tpu as pltpu
from jax.sharding import PartitionSpec as P

P_SIZE = 1048576
MESH = pl.DeviceIdType.MESH
HIGHEST = lax.Precision.HIGHEST
Y, ZH, ZL, X, C = 4, 4, 4, 4, 2
GROUPS, PLANE, LINE = Y * ZH, Y * X * C, ZH * ZL
EARLY = 1


def turn(a, b, n):
    return lax.rem(a + b, n)


def kernel(width_ref, x_ref, s_ref, repel_ref, drive_ref, xs, ss, pulls, drives, parts, scattered, lined, gathered,
           own, x_send, x_recv, s_send, s_recv, r_send, r_recv, d_send, d_recv,
           a_send, a_recv, b_send, b_recv, c_send, c_recv):
    g, p = lax.axis_index("grp"), lax.axis_index("par")
    y, zh = lax.div(g, ZH), lax.rem(g, ZH)
    zl, x, c = lax.div(p, X * C), lax.rem(lax.div(p, C), X), lax.rem(p, C)
    plane = (y * X + x) * C + c
    line = zh * ZL + zl
    rows, cols = xs.shape[1], xs.shape[2]

    def group_peer(k):
        return turn(y, lax.div(k, ZH), Y) * ZH + turn(zh, lax.rem(k, ZH), ZH)

    def plane_peer(k):
        py, px = turn(y, lax.div(k, X * C), Y), turn(x, lax.rem(lax.div(k, C), X), X)
        pc = turn(c, lax.rem(k, C), C)
        return (py * X + px) * C + pc, {"grp": py * ZH + zh, "par": zl * (X * C) + px * C + pc}

    def line_peer(k):
        ph, pz = turn(zh, lax.div(k, ZL), ZH), turn(zl, lax.rem(k, ZL), ZL)
        return {"grp": y * ZH + ph, "par": pz * (X * C) + x * C + c}

    def columns(q):
        return pl.ds(pl.multiple_of(q * cols, cols), cols)

    def each(low, high, body):
        lax.fori_loop(low, high, lambda k, _: (body(k), None)[1], None)

    barrier = pltpu.get_barrier_semaphore()

    def greet(where):
        pl.semaphore_signal(barrier, inc=1, device_id=where, device_id_type=MESH)

    each(1, GROUPS, lambda k: greet({"grp": group_peer(k)}))
    each(1, LINE, lambda k: greet(line_peer(k)))
    each(1, PLANE, lambda k: greet(plane_peer(k)[1]))
    pl.semaphore_wait(barrier, GROUPS + LINE + PLANE - 3)

    def bring(src, dst, send, recv):
        def copy(k):
            q = group_peer(k)
            return pltpu.make_async_remote_copy(
                src_ref=src.at[:, columns(q)], dst_ref=dst.at[g], send_sem=send.at[k], recv_sem=recv.at[k],
                device_id={"grp": q}, device_id_type=MESH)
        return copy

    def give(src, dst, send, recv):
        def copy(k):
            q = group_peer(k)
            return pltpu.make_async_remote_copy(
                src_ref=src.at[q], dst_ref=dst.at[:, columns(g)], send_sem=send.at[k], recv_sem=recv.at[k],
                device_id={"grp": q}, device_id_type=MESH)
        return copy

    x_in, s_in = bring(x_ref, xs, x_send, x_recv), bring(s_ref, ss, s_send, s_recv)
    r_out, d_out = give(pulls, repel_ref, r_send, r_recv), give(drives, drive_ref, d_send, d_recv)
    own_x = pltpu.make_async_copy(x_ref.at[:, columns(g)], xs.at[g], own.at[0])
    own_s = pltpu.make_async_copy(s_ref.at[:, columns(g)], ss.at[g], own.at[1])

    each(1, GROUPS, lambda k: x_in(k).start())
    own_x.start()
    own_s.start()
    each(1, ZH * EARLY, lambda k: s_in(k).start())

    own_x.wait()
    each(1, GROUPS, lambda k: x_in(k).wait_recv())
    block = xs[...].reshape(GROUPS * rows, cols)
    inner = lax.dot_general(block, block, (((1,), (1,)), ((), ())), precision=HIGHEST, preferred_element_type=jnp.float32)
    n = GROUPS * rows
    same = lax.broadcasted_iota(jnp.int32, (n, n), 0) == lax.broadcasted_iota(jnp.int32, (n, n), 1)
    norms = jnp.where(same, inner, 0.0)
    part = jnp.sum(norms, axis=1, keepdims=True) + jnp.sum(norms, axis=0, keepdims=True) - 2.0 * inner
    parts[...] = jnp.concatenate([part[: n // 2], part[n // 2 :]], axis=1).reshape(parts.shape)

    def scatter(k):
        q, where = plane_peer(k)
        return pltpu.make_async_remote_copy(
            src_ref=parts.at[q], dst_ref=scattered.at[plane], send_sem=a_send.at[k], recv_sem=a_recv.at[k],
            device_id=where, device_id_type=MESH)

    def along(k):
        return pltpu.make_async_remote_copy(
            src_ref=lined.at[line], dst_ref=lined.at[line], send_sem=b_send.at[k], recv_sem=b_recv.at[k],
            device_id=line_peer(k), device_id_type=MESH)

    def gather(k):
        return pltpu.make_async_remote_copy(
            src_ref=gathered.at[plane], dst_ref=gathered.at[plane], send_sem=c_send.at[k], recv_sem=c_recv.at[k],
            device_id=plane_peer(k)[1], device_id_type=MESH)

    each(1, PLANE, lambda k: scatter(k).start())
    scattered[plane] = parts[plane]
    each(1, PLANE, lambda k: scatter(k).wait_recv())
    lined[line] = jnp.sum(scattered[...], axis=0)
    each(1, LINE, lambda k: along(k).start())
    each(ZH * EARLY, GROUPS, lambda k: s_in(k).start())
    each(1, LINE, lambda k: along(k).wait_recv())
    gathered[plane] = jnp.sum(lined[...], axis=0)
    each(1, PLANE, lambda k: gather(k).start())
    each(1, PLANE, lambda k: gather(k).wait_recv())

    width = width_ref[0]
    both = gathered[...].reshape(n // 2, 2 * n)
    dist = jnp.concatenate([both[:, :n], both[:, n:]], axis=0)
    kern = jnp.exp(-dist / (width * P_SIZE))
    weight = jnp.sum(kern, axis=1, keepdims=True)
    block = xs[...].reshape(n, cols)
    pull = jnp.dot(kern, block, precision=HIGHEST, preferred_element_type=jnp.float32)
    pulls[...] = ((block * weight - pull) / (n * width)).reshape(pulls.shape)
    each(1, GROUPS, lambda k: r_out(k).start())
    own_r = pltpu.make_async_copy(pulls.at[g], repel_ref.at[:, columns(g)], own.at[2])
    own_r.start()

    own_s.wait()
    each(1, GROUPS, lambda k: s_in(k).wait_recv())
    block = ss[...].reshape(n, cols)
    drive = jnp.dot(kern, block, precision=HIGHEST, preferred_element_type=jnp.float32)
    drives[...] = (drive / n).reshape(drives.shape)
    each(1, GROUPS, lambda k: d_out(k).start())
    own_d = pltpu.make_async_copy(drives.at[g], drive_ref.at[:, columns(g)], own.at[3])
    own_d.start()

    each(1, GROUPS, lambda k: (x_in(k).wait_send(), s_in(k).wait_send()))
    each(1, PLANE, lambda k: (scatter(k).wait_send(), gather(k).wait_send()))
    each(1, LINE, lambda k: along(k).wait_send())
    own_r.wait()
    own_d.wait()
    each(1, GROUPS, lambda k: r_out(k).wait())
    each(1, GROUPS, lambda k: d_out(k).wait())


def shards(particles, scores, kernel_width):
    rows, length = particles.shape
    cols = length // GROUPS
    n = GROUPS * rows
    whole = pltpu.VMEM((GROUPS, rows, cols), jnp.float32)
    piece = n * n // PLANE
    out = jax.ShapeDtypeStruct(particles.shape, jnp.float32)
    dma = pltpu.SemaphoreType.DMA
    repel, drive = pl.pallas_call(
        kernel,
        out_shape=(out, out),
        in_specs=[pl.BlockSpec(memory_space=pltpu.SMEM)] + [pl.BlockSpec(memory_space=pl.ANY)] * 2,
        out_specs=(pl.BlockSpec(memory_space=pl.ANY),) * 2,
        scratch_shapes=[whole] * 4
        + [pltpu.VMEM((k, 1, piece), jnp.float32) for k in (PLANE, PLANE, LINE, PLANE)]
        + [dma((4,))] + [dma((GROUPS,))] * 8 + [dma((PLANE,))] * 2 + [dma((LINE,))] * 2 + [dma((PLANE,))] * 2,
        compiler_params=pltpu.CompilerParams(collective_id=0, has_side_effects=True, vmem_limit_bytes=24 << 20),
    )(kernel_width, particles, scores)
    return (drive, repel)


def solution(mesh):
    return jax.shard_map(
        shards,
        mesh=mesh,
        in_specs=(P("grp", "par"), P("grp", "par"), P()),
        out_specs=(P("grp", "par"), P("grp", "par")),
        check_vma=False,
    )
```

time: 245 us -> 128 us (0.52)
  the two profiles are of different devices: /device:TPU:1 before, /device:TPU:64 now
where the time goes in v2:
time: 128 us
  Pallas kernels  123 us (96%)
  local copies, waits for them, and re-layouts  3.66 us (3%)
  between operations  1.29 us (1%)
    pallas_call x1, Pallas kernels, shards(): pl.pallas_call(kernel, out_shape=(out, out), in_specs=[pl.BlockSpec(memor...  123 us
    unnamed x6, local copies, waits for them, and re-layouts  3.66 us

profile of v2, /device:TPU:64, one launch (start us, length us, event | category | flops | bytes accessed | tf_op | source)
XLA Modules:
  0.0 128.3 jit_solution(15358255249088655249)
XLA Ops:
  1.3 0.0 copy-start
  1.3 1.0 copy-done
  2.3 0.0 copy-start.1
  2.3 1.0 copy-done.1
  3.4 123.3 %shard_map.50 = (f32[4,32768]{1,0:T(4,128)S(1)}, f32[4,32768]{1,0:T(4,128)S(1)}) custom-call(f32[1]{0:T(128)S(6)} %copy.7.width_ref, f32[4,32768]{1,0:T(4,128)S(1)} %copy-done, f32[4,32768]{1,0:T(4,128)S(1)} %copy-done.1), custom_call_target="tpu_custom_call" | custom-call | tf_op jit(solution)/shard_map/pallas_call | solution.py:159
  126.7 0.8 copy.8
  127.5 0.8 copy.9
Async XLA Ops:
  1.3 1.0 copy-start
  2.3 1.0 copy-start.1

commit v3 on v2

--- a/solution.py
+++ b/solution.py
@@ -17,9 +17,8 @@
     return lax.rem(a + b, n)
 
 
-def kernel(width_ref, x_ref, s_ref, repel_ref, drive_ref, xs, ss, pulls, drives, parts, scattered, lined, gathered,
-           own, x_send, x_recv, s_send, s_recv, r_send, r_recv, d_send, d_recv,
-           a_send, a_recv, b_send, b_recv, c_send, c_recv):
+def kernel(width_hbm, x_ref, s_ref, repel_ref, drive_ref, xs, ss, pulls, drives, parts, scattered, lined, gathered,
+           width_ref, own, x_sem, s_sem, r_sem, d_sem, a_sem, b_sem, c_sem):
     g, p = lax.axis_index("grp"), lax.axis_index("par")
     y, zh = lax.div(g, ZH), lax.rem(g, ZH)
     zl, x, c = lax.div(p, X * C), lax.rem(lax.div(p, C), X), lax.rem(p, C)
@@ -55,34 +54,40 @@
     each(1, PLANE, lambda k: greet(plane_peer(k)[1]))
     pl.semaphore_wait(barrier, GROUPS + LINE + PLANE - 3)
 
-    def bring(src, dst, send, recv):
+    def bring(src, dst, sem):
         def copy(k):
             q = group_peer(k)
             return pltpu.make_async_remote_copy(
-                src_ref=src.at[:, columns(q)], dst_ref=dst.at[g], send_sem=send.at[k], recv_sem=recv.at[k],
+                src_ref=src.at[:, columns(q)], dst_ref=dst.at[g], send_sem=sem.at[0], recv_sem=sem.at[1],
                 device_id={"grp": q}, device_id_type=MESH)
         return copy
 
-    def give(src, dst, send, recv):
+    def give(src, dst, sem):
         def copy(k):
             q = group_peer(k)
             return pltpu.make_async_remote_copy(
-                src_ref=src.at[q], dst_ref=dst.at[:, columns(g)], send_sem=send.at[k], recv_sem=recv.at[k],
+                src_ref=src.at[q], dst_ref=dst.at[:, columns(g)], send_sem=sem.at[0], recv_sem=sem.at[1],
                 device_id={"grp": q}, device_id_type=MESH)
         return copy
 
-    x_in, s_in = bring(x_ref, xs, x_send, x_recv), bring(s_ref, ss, s_send, s_recv)
-    r_out, d_out = give(pulls, repel_ref, r_send, r_recv), give(drives, drive_ref, d_send, d_recv)
+    def await_all(buffer, count, sem):
+        whole = buffer.at[pl.ds(0, count)]
+        pltpu.make_async_copy(whole, whole, sem).wait()
+
+    x_in, s_in = bring(x_ref, xs, x_sem), bring(s_ref, ss, s_sem)
+    r_out, d_out = give(pulls, repel_ref, r_sem), give(drives, drive_ref, d_sem)
+    get_width = pltpu.make_async_copy(width_hbm, width_ref, own.at[4])
     own_x = pltpu.make_async_copy(x_ref.at[:, columns(g)], xs.at[g], own.at[0])
     own_s = pltpu.make_async_copy(s_ref.at[:, columns(g)], ss.at[g], own.at[1])
 
     each(1, GROUPS, lambda k: x_in(k).start())
     own_x.start()
     own_s.start()
+    get_width.start()
     each(1, ZH * EARLY, lambda k: s_in(k).start())
 
     own_x.wait()
-    each(1, GROUPS, lambda k: x_in(k).wait_recv())
+    await_all(xs, GROUPS - 1, x_sem.at[1])
     block = xs[...].reshape(GROUPS * rows, cols)
     inner = lax.dot_general(block, block, (((1,), (1,)), ((), ())), precision=HIGHEST, preferred_element_type=jnp.float32)
     n = GROUPS * rows
@@ -94,30 +99,31 @@
     def scatter(k):
         q, where = plane_peer(k)
         return pltpu.make_async_remote_copy(
-            src_ref=parts.at[q], dst_ref=scattered.at[plane], send_sem=a_send.at[k], recv_sem=a_recv.at[k],
+            src_ref=parts.at[q], dst_ref=scattered.at[plane], send_sem=a_sem.at[0], recv_sem=a_sem.at[1],
             device_id=where, device_id_type=MESH)
 
     def along(k):
         return pltpu.make_async_remote_copy(
-            src_ref=lined.at[line], dst_ref=lined.at[line], send_sem=b_send.at[k], recv_sem=b_recv.at[k],
+            src_ref=lined.at[line], dst_ref=lined.at[line], send_sem=b_sem.at[0], recv_sem=b_sem.at[1],
             device_id=line_peer(k), device_id_type=MESH)
 
     def gather(k):
         return pltpu.make_async_remote_copy(
-            src_ref=gathered.at[plane], dst_ref=gathered.at[plane], send_sem=c_send.at[k], recv_sem=c_recv.at[k],
+            src_ref=gathered.at[plane], dst_ref=gathered.at[plane], send_sem=c_sem.at[0], recv_sem=c_sem.at[1],
             device_id=plane_peer(k)[1], device_id_type=MESH)
 
     each(1, PLANE, lambda k: scatter(k).start())
     scattered[plane] = parts[plane]
-    each(1, PLANE, lambda k: scatter(k).wait_recv())
+    await_all(scattered, PLANE - 1, a_sem.at[1])
     lined[line] = jnp.sum(scattered[...], axis=0)
     each(1, LINE, lambda k: along(k).start())
     each(ZH * EARLY, GROUPS, lambda k: s_in(k).start())
-    each(1, LINE, lambda k: along(k).wait_recv())
+    await_all(lined, LINE - 1, b_sem.at[1])
     gathered[plane] = jnp.sum(lined[...], axis=0)
     each(1, PLANE, lambda k: gather(k).start())
-    each(1, PLANE, lambda k: gather(k).wait_recv())
+    await_all(gathered, PLANE - 1, c_sem.at[1])
 
+    get_width.wait()
     width = width_ref[0]
     both = gathered[...].reshape(n // 2, 2 * n)
     dist = jnp.concatenate([both[:, :n], both[:, n:]], axis=0)
@@ -131,7 +137,7 @@
     own_r.start()
 
     own_s.wait()
-    each(1, GROUPS, lambda k: s_in(k).wait_recv())
+    await_all(ss, GROUPS - 1, s_sem.at[1])
     block = ss[...].reshape(n, cols)
     drive = jnp.dot(kern, block, precision=HIGHEST, preferred_element_type=jnp.float32)
     drives[...] = (drive / n).reshape(drives.shape)
@@ -139,13 +145,16 @@
     own_d = pltpu.make_async_copy(drives.at[g], drive_ref.at[:, columns(g)], own.at[3])
     own_d.start()
 
-    each(1, GROUPS, lambda k: (x_in(k).wait_send(), s_in(k).wait_send()))
-    each(1, PLANE, lambda k: (scatter(k).wait_send(), gather(k).wait_send()))
-    each(1, LINE, lambda k: along(k).wait_send())
+    await_all(xs, GROUPS - 1, x_sem.at[0])
+    await_all(ss, GROUPS - 1, s_sem.at[0])
+    await_all(parts, PLANE - 1, a_sem.at[0])
+    await_all(lined, LINE - 1, b_sem.at[0])
+    await_all(gathered, PLANE - 1, c_sem.at[0])
     own_r.wait()
     own_d.wait()
-    each(1, GROUPS, lambda k: r_out(k).wait())
-    each(1, GROUPS, lambda k: d_out(k).wait())
+    for sem in (r_sem, d_sem):
+        await_all(pulls, GROUPS - 1, sem.at[0])
+        await_all(pulls, GROUPS - 1, sem.at[1])
 
 
 def shards(particles, scores, kernel_width):
@@ -159,12 +168,12 @@
     repel, drive = pl.pallas_call(
         kernel,
         out_shape=(out, out),
-        in_specs=[pl.BlockSpec(memory_space=pltpu.SMEM)] + [pl.BlockSpec(memory_space=pl.ANY)] * 2,
-        out_specs=(pl.BlockSpec(memory_space=pl.ANY),) * 2,
+        in_specs=[pl.BlockSpec(memory_space=pl.ANY)] * 3,
+        out_specs=(pl.BlockSpec(memory_space=pltpu.VMEM),) * 2,
         scratch_shapes=[whole] * 4
         + [pltpu.VMEM((k, 1, piece), jnp.float32) for k in (PLANE, PLANE, LINE, PLANE)]
-        + [dma((4,))] + [dma((GROUPS,))] * 8 + [dma((PLANE,))] * 2 + [dma((LINE,))] * 2 + [dma((PLANE,))] * 2,
-        compiler_params=pltpu.CompilerParams(collective_id=0, has_side_effects=True, vmem_limit_bytes=24 << 20),
+        + [pltpu.SMEM((1,), jnp.float32), dma((5,))] + [dma((2,))] * 7,
+        compiler_params=pltpu.CompilerParams(collective_id=0, has_side_effects=True, vmem_limit_bytes=55050240),
     )(kernel_width, particles, scores)
     return (drive, repel)
 

time: 128 us -> 125 us (0.977)
  the two profiles are of different devices: /device:TPU:64 before, /device:TPU:1 now
where the time goes in v3:
time: 125 us; the launch traced here: 122 us
  Pallas kernels  119 us (95%)
  local copies, waits for them, and re-layouts  1.59 us (1%)
  between operations  1.29 us (1%)
    pallas_call x1, Pallas kernels, shards(): pl.pallas_call(kernel, out_shape=(out, out), in_specs=[pl.BlockSpec(memor...  119 us

profile of v3, /device:TPU:1, one launch (start us, length us, event | category | flops | bytes accessed | tf_op | source)
XLA Modules:
  0.0 122.2 jit_solution(16039045597826818244)
XLA Ops:
  1.3 119.3 %shard_map.50 = (f32[4,32768]{1,0:T(4,128)S(1)}, f32[4,32768]{1,0:T(4,128)S(1)}) custom-call(f32[1]{0:T(128)S(6)} %copy.7.width_hbm, f32[4,32768]{1,0:T(4,128)} %x_ref.1, f32[4,32768]{1,0:T(4,128)} %s_ref.1), custom_call_target="tpu_custom_call" | custom-call | tf_op jit(solution)/shard_map/pallas_call | solution.py:168
  120.6 0.8 copy.8
  121.4 0.8 copy.9

commit v4 on v3

--- a/solution.py
+++ b/solution.py
@@ -9,8 +9,7 @@
 MESH = pl.DeviceIdType.MESH
 HIGHEST = lax.Precision.HIGHEST
 Y, ZH, ZL, X, C = 4, 4, 4, 4, 2
-GROUPS, PLANE, LINE = Y * ZH, Y * X * C, ZH * ZL
-EARLY = 1
+GROUPS, PLANE, LINE, OWNERS = Y * ZH, Y * X * C, ZH * ZL, Y * X
 
 
 def turn(a, b, n):
@@ -23,7 +22,7 @@
     y, zh = lax.div(g, ZH), lax.rem(g, ZH)
     zl, x, c = lax.div(p, X * C), lax.rem(lax.div(p, C), X), lax.rem(p, C)
     plane = (y * X + x) * C + c
-    line = zh * ZL + zl
+    owner, line = y * X + x, zh * ZL + zl
     rows, cols = xs.shape[1], xs.shape[2]
 
     def group_peer(k):
@@ -34,6 +33,10 @@
         pc = turn(c, lax.rem(k, C), C)
         return (py * X + px) * C + pc, {"grp": py * ZH + zh, "par": zl * (X * C) + px * C + pc}
 
+    def owner_peer(k):
+        py, px = turn(y, lax.div(k, X), Y), turn(x, lax.rem(k, X), X)
+        return py * X + px, {"grp": py * ZH + zh, "par": zl * (X * C) + px * C}
+
     def line_peer(k):
         ph, pz = turn(zh, lax.div(k, ZL), ZH), turn(zl, lax.rem(k, ZL), ZL)
         return {"grp": y * ZH + ph, "par": pz * (X * C) + x * C + c}
@@ -50,9 +53,17 @@
         pl.semaphore_signal(barrier, inc=1, device_id=where, device_id_type=MESH)
 
     each(1, GROUPS, lambda k: greet({"grp": group_peer(k)}))
-    each(1, LINE, lambda k: greet(line_peer(k)))
-    each(1, PLANE, lambda k: greet(plane_peer(k)[1]))
-    pl.semaphore_wait(barrier, GROUPS + LINE + PLANE - 3)
+
+    @pl.when(c == 0)
+    def _():
+        each(1, LINE, lambda k: greet(line_peer(k)))
+        each(1, PLANE, lambda k: greet(plane_peer(k)[1]))
+        pl.semaphore_wait(barrier, GROUPS + LINE + PLANE - 3)
+
+    @pl.when(c != 0)
+    def _():
+        each(0, OWNERS, lambda k: greet(owner_peer(k)[1]))
+        pl.semaphore_wait(barrier, GROUPS + OWNERS - 1)
 
     def bring(src, dst, sem):
         def copy(k):
@@ -84,8 +95,6 @@
     own_x.start()
     own_s.start()
     get_width.start()
-    each(1, ZH * EARLY, lambda k: s_in(k).start())
-
     own_x.wait()
     await_all(xs, GROUPS - 1, x_sem.at[1])
     block = xs[...].reshape(GROUPS * rows, cols)
@@ -97,7 +106,7 @@
     parts[...] = jnp.concatenate([part[: n // 2], part[n // 2 :]], axis=1).reshape(parts.shape)
 
     def scatter(k):
-        q, where = plane_peer(k)
+        q, where = owner_peer(k)
         return pltpu.make_async_remote_copy(
             src_ref=parts.at[q], dst_ref=scattered.at[plane], send_sem=a_sem.at[0], recv_sem=a_sem.at[1],
             device_id=where, device_id_type=MESH)
@@ -109,19 +118,34 @@
 
     def gather(k):
         return pltpu.make_async_remote_copy(
-            src_ref=gathered.at[plane], dst_ref=gathered.at[plane], send_sem=c_sem.at[0], recv_sem=c_sem.at[1],
+            src_ref=gathered.at[owner], dst_ref=gathered.at[owner], send_sem=c_sem.at[0], recv_sem=c_sem.at[1],
             device_id=plane_peer(k)[1], device_id_type=MESH)
 
-    each(1, PLANE, lambda k: scatter(k).start())
-    scattered[plane] = parts[plane]
-    await_all(scattered, PLANE - 1, a_sem.at[1])
-    lined[line] = jnp.sum(scattered[...], axis=0)
-    each(1, LINE, lambda k: along(k).start())
-    each(ZH * EARLY, GROUPS, lambda k: s_in(k).start())
-    await_all(lined, LINE - 1, b_sem.at[1])
-    gathered[plane] = jnp.sum(lined[...], axis=0)
-    each(1, PLANE, lambda k: gather(k).start())
-    await_all(gathered, PLANE - 1, c_sem.at[1])
+    each(OWNERS // 2, OWNERS, lambda k: scatter(k).start())
+    each(1 - c, OWNERS // 2, lambda k: scatter(k).start())
+
+    @pl.when(c != 0)
+    def _():
+        each(1, GROUPS, lambda k: s_in(k).start())
+
+
+    @pl.when(c == 0)
+    def _():
+        scattered[plane] = parts[owner]
+        await_all(scattered, PLANE - 1, a_sem.at[1])
+        lined[line] = jnp.sum(scattered[...], axis=0)
+        each(LINE // 2, LINE, lambda k: along(k).start())
+        each(1, LINE // 2, lambda k: along(k).start())
+        each(1, GROUPS, lambda k: s_in(k).start())
+        await_all(lined, LINE - 1, b_sem.at[1])
+        gathered[owner] = jnp.sum(lined[...], axis=0)
+        each(PLANE // 2, PLANE, lambda k: gather(k).start())
+        each(1, PLANE // 2, lambda k: gather(k).start())
+        await_all(gathered, OWNERS - 1, c_sem.at[1])
+
+    @pl.when(c != 0)
+    def _():
+        await_all(gathered, OWNERS, c_sem.at[1])
 
     get_width.wait()
     width = width_ref[0]
@@ -147,9 +171,17 @@
 
     await_all(xs, GROUPS - 1, x_sem.at[0])
     await_all(ss, GROUPS - 1, s_sem.at[0])
-    await_all(parts, PLANE - 1, a_sem.at[0])
-    await_all(lined, LINE - 1, b_sem.at[0])
-    await_all(gathered, PLANE - 1, c_sem.at[0])
+
+    @pl.when(c == 0)
+    def _():
+        await_all(parts, OWNERS - 1, a_sem.at[0])
+        await_all(lined, LINE - 1, b_sem.at[0])
+        await_all(scattered, PLANE - 1, c_sem.at[0])
+
+    @pl.when(c != 0)
+    def _():
+        await_all(parts, OWNERS, a_sem.at[0])
+
     own_r.wait()
     own_d.wait()
     for sem in (r_sem, d_sem):
@@ -162,7 +194,7 @@
     cols = length // GROUPS
     n = GROUPS * rows
     whole = pltpu.VMEM((GROUPS, rows, cols), jnp.float32)
-    piece = n * n // PLANE
+    piece = (n * n // (OWNERS * 2 * n), 2 * n)
     out = jax.ShapeDtypeStruct(particles.shape, jnp.float32)
     dma = pltpu.SemaphoreType.DMA
     repel, drive = pl.pallas_call(
@@ -171,7 +203,7 @@
         in_specs=[pl.BlockSpec(memory_space=pl.ANY)] * 3,
         out_specs=(pl.BlockSpec(memory_space=pltpu.VMEM),) * 2,
         scratch_shapes=[whole] * 4
-        + [pltpu.VMEM((k, 1, piece), jnp.float32) for k in (PLANE, PLANE, LINE, PLANE)]
+        + [pltpu.VMEM((k, *piece), jnp.float32) for k in (OWNERS, PLANE, LINE, OWNERS)]
         + [pltpu.SMEM((1,), jnp.float32), dma((5,))] + [dma((2,))] * 7,
         compiler_params=pltpu.CompilerParams(collective_id=0, has_side_effects=True, vmem_limit_bytes=55050240),
     )(kernel_width, particles, scores)

time: 125 us -> 122 us (0.976); the launches traced: 122 us -> 121 us
  no operation moved by 1% of the time
where the time goes in v4:
time: 122 us; the launch traced here: 121 us
  Pallas kernels  118 us (97%)
  local copies, waits for them, and re-layouts  1.59 us (1%)
  between operations  1.29 us (1%)
    pallas_call x1, Pallas kernels, shards(): pl.pallas_call(kernel, out_shape=(out, out), in_specs=[pl.BlockSpec(memor...  118 us

profile of v4, /device:TPU:1, one launch (start us, length us, event | category | flops | bytes accessed | tf_op | source)
XLA Modules:
  0.0 121.3 jit_solution(10727341740371867418)
XLA Ops:
  1.3 118.4 %shard_map.50 = (f32[4,32768]{1,0:T(4,128)S(1)}, f32[4,32768]{1,0:T(4,128)S(1)}) custom-call(f32[1]{0:T(128)S(6)} %copy.7.width_hbm, f32[4,32768]{1,0:T(4,128)} %x_ref.1, f32[4,32768]{1,0:T(4,128)} %s_ref.1), custom_call_target="tpu_custom_call" | custom-call | tf_op jit(solution)/shard_map/pallas_call | solution.py:200
  119.7 0.8 copy.8
  120.5 0.8 copy.9

commit v5 on v4

--- a/solution.py
+++ b/solution.py
@@ -17,13 +17,18 @@
 
 
 def kernel(width_hbm, x_ref, s_ref, repel_ref, drive_ref, xs, ss, pulls, drives, parts, scattered, lined, gathered,
-           width_ref, own, x_sem, s_sem, r_sem, d_sem, a_sem, b_sem, c_sem):
+           width_ref, own, x_sem, r_sem, d_sem, a_sem, b_sem, c_sem, ts, twin_drives, t_sem):
     g, p = lax.axis_index("grp"), lax.axis_index("par")
     y, zh = lax.div(g, ZH), lax.rem(g, ZH)
     zl, x, c = lax.div(p, X * C), lax.rem(lax.div(p, C), X), lax.rem(p, C)
     plane = (y * X + x) * C + c
     owner, line = y * X + x, zh * ZL + zl
     rows, cols = xs.shape[1], xs.shape[2]
+
+    def at(dy, dz):
+        return turn(y, dy, Y) * ZH + turn(zh, dz, ZH)
+
+    elder = at(0, ZH - 1)
 
     def group_peer(k):
         return turn(y, lax.div(k, ZH), Y) * ZH + turn(zh, lax.rem(k, ZH), ZH)
@@ -85,16 +90,46 @@
         whole = buffer.at[pl.ds(0, count)]
         pltpu.make_async_copy(whole, whole, sem).wait()
 
-    x_in, s_in = bring(x_ref, xs, x_sem), bring(s_ref, ss, s_sem)
-    r_out, d_out = give(pulls, repel_ref, r_sem), give(drives, drive_ref, d_sem)
+    x_in, r_out = bring(x_ref, xs, x_sem), give(pulls, repel_ref, r_sem)
     get_width = pltpu.make_async_copy(width_hbm, width_ref, own.at[4])
     own_x = pltpu.make_async_copy(x_ref.at[:, columns(g)], xs.at[g], own.at[0])
     own_s = pltpu.make_async_copy(s_ref.at[:, columns(g)], ss.at[g], own.at[1])
+
+    def send(src, dst, where, send_sem, recv_sem):
+        return pltpu.make_async_remote_copy(
+            src_ref=src, dst_ref=dst, send_sem=t_sem.at[send_sem], recv_sem=t_sem.at[recv_sem],
+            device_id={"grp": where}, device_id_type=MESH)
+
+    def to_owner(dy, dz, recv):
+        q = at(dy, dz)
+        send(s_ref.at[:, columns(q)], ss.at[g], q, 0, recv).start()
+
+    def to_twin(dy, dz, recv):
+        send(s_ref.at[:, columns(at(dy, dz))], ts.at[g], at(dy, dz + 1), 1, recv).start()
+
+    def on_to_twin(dy):
+        h = at(dy, ZH - 1)
+        send(ss.at[h], ts.at[h], at(0, 1), 2, 7).start()
+
+    def on_to_owner(dy):
+        h = at(dy, 1)
+        send(ts.at[h], ss.at[h], elder, 2, 8).start()
+
+    own_t = pltpu.make_async_copy(s_ref.at[:, columns(elder)], ts.at[g], own.at[5])
+    own_e = pltpu.make_async_copy(twin_drives.at[g], drive_ref.at[:, columns(elder)], own.at[6])
 
     each(1, GROUPS, lambda k: x_in(k).start())
     own_x.start()
     own_s.start()
     get_width.start()
+    own_t.start()
+
+    @pl.when(c != 0)
+    def _():
+        each(0, Y, lambda k: to_owner(k, 1, 3))
+        each(0, Y, lambda k: to_twin(k, 2, 4))
+
+
     own_x.wait()
     await_all(xs, GROUPS - 1, x_sem.at[1])
     block = xs[...].reshape(GROUPS * rows, cols)
@@ -124,9 +159,13 @@
     each(OWNERS // 2, OWNERS, lambda k: scatter(k).start())
     each(1 - c, OWNERS // 2, lambda k: scatter(k).start())
 
-    @pl.when(c != 0)
-    def _():
-        each(1, GROUPS, lambda k: s_in(k).start())
+
+    @pl.when(c != 0)
+    def _():
+        each(0, Y, lambda k: to_owner(k, 3, 5))
+        each(0, Y, lambda k: to_twin(k, 0, 6))
+        each(1, Y, lambda k: to_owner(k, 0, 5))
+        each(1, Y, lambda k: to_twin(k, 3, 6))
 
 
     @pl.when(c == 0)
@@ -136,15 +175,28 @@
         lined[line] = jnp.sum(scattered[...], axis=0)
         each(LINE // 2, LINE, lambda k: along(k).start())
         each(1, LINE // 2, lambda k: along(k).start())
-        each(1, GROUPS, lambda k: s_in(k).start())
+        each(0, Y, lambda k: to_owner(k, 1, 3))
+        each(0, Y, lambda k: to_twin(k, 2, 4))
+        each(0, Y, lambda k: to_owner(k, 3, 5))
+        each(0, Y, lambda k: to_twin(k, 0, 6))
+        each(1, Y, lambda k: to_owner(k, 0, 5))
+        each(1, Y, lambda k: to_twin(k, 3, 6))
         await_all(lined, LINE - 1, b_sem.at[1])
         gathered[owner] = jnp.sum(lined[...], axis=0)
         each(PLANE // 2, PLANE, lambda k: gather(k).start())
         each(1, PLANE // 2, lambda k: gather(k).start())
+        await_all(ss, Y, t_sem.at[3])
+        each(0, Y, on_to_twin)
+        await_all(ts, Y, t_sem.at[4])
+        each(0, Y, on_to_owner)
         await_all(gathered, OWNERS - 1, c_sem.at[1])
 
     @pl.when(c != 0)
     def _():
+        await_all(ss, Y, t_sem.at[3])
+        each(0, Y, on_to_twin)
+        await_all(ts, Y, t_sem.at[4])
+        each(0, Y, on_to_owner)
         await_all(gathered, OWNERS, c_sem.at[1])
 
     get_width.wait()
@@ -161,16 +213,44 @@
     own_r.start()
 
     own_s.wait()
-    await_all(ss, GROUPS - 1, s_sem.at[1])
-    block = ss[...].reshape(n, cols)
-    drive = jnp.dot(kern, block, precision=HIGHEST, preferred_element_type=jnp.float32)
-    drives[...] = (drive / n).reshape(drives.shape)
-    each(1, GROUPS, lambda k: d_out(k).start())
+    await_all(ss, 2 * Y - 1, t_sem.at[5])
+    await_all(ss, Y, t_sem.at[8])
+
+    def driven(scores):
+        block = scores[...].reshape(n, cols)
+        drive = jnp.dot(kern, block, precision=HIGHEST, preferred_element_type=jnp.float32)
+        return (drive / n).reshape(drives.shape)
+
+    drives[...] = driven(ss)
+
+    def back(src, piece, dy, dz):
+        q = at(dy, dz)
+        pltpu.make_async_remote_copy(
+            src_ref=src.at[q], dst_ref=drive_ref.at[:, columns(piece)], send_sem=d_sem.at[0], recv_sem=d_sem.at[1],
+            device_id={"grp": q}, device_id_type=MESH).start()
+
+    each(0, Y, lambda k: back(drives, g, k, ZH - 1))
+    own_t.wait()
+    await_all(ts, 2 * Y - 1, t_sem.at[6])
+    await_all(ts, Y, t_sem.at[7])
+    twin_drives[...] = driven(ts)
+    each(0, Y, lambda k: back(twin_drives, elder, k, 1))
+    each(1, Y, lambda k: back(drives, g, k, 0))
+    each(1, Y, lambda k: back(twin_drives, elder, k, 0))
+    own_e.start()
     own_d = pltpu.make_async_copy(drives.at[g], drive_ref.at[:, columns(g)], own.at[3])
     own_d.start()
 
     await_all(xs, GROUPS - 1, x_sem.at[0])
-    await_all(ss, GROUPS - 1, s_sem.at[0])
+    own_r.wait()
+    own_d.wait()
+
+    own_e.wait()
+    await_all(ss, 3 * Y - 1, t_sem.at[0])
+    await_all(ts, 3 * Y - 1, t_sem.at[1])
+    await_all(ss, 2 * Y, t_sem.at[2])
+    await_all(pulls, GROUPS - 2, d_sem.at[0])
+    await_all(pulls, GROUPS - 2, d_sem.at[1])
 
     @pl.when(c == 0)
     def _():
@@ -182,11 +262,8 @@
     def _():
         await_all(parts, OWNERS, a_sem.at[0])
 
-    own_r.wait()
-    own_d.wait()
-    for sem in (r_sem, d_sem):
-        await_all(pulls, GROUPS - 1, sem.at[0])
-        await_all(pulls, GROUPS - 1, sem.at[1])
+    await_all(pulls, GROUPS - 1, r_sem.at[0])
+    await_all(pulls, GROUPS - 1, r_sem.at[1])
 
 
 def shards(particles, scores, kernel_width):
@@ -204,7 +281,7 @@
         out_specs=(pl.BlockSpec(memory_space=pltpu.VMEM),) * 2,
         scratch_shapes=[whole] * 4
         + [pltpu.VMEM((k, *piece), jnp.float32) for k in (OWNERS, PLANE, LINE, OWNERS)]
-        + [pltpu.SMEM((1,), jnp.float32), dma((5,))] + [dma((2,))] * 7,
+        + [pltpu.SMEM((1,), jnp.float32), dma((7,))] + [dma((2,))] * 6 + [whole] * 2 + [dma((9,))],
         compiler_params=pltpu.CompilerParams(collective_id=0, has_side_effects=True, vmem_limit_bytes=55050240),
     )(kernel_width, particles, scores)
     return (drive, repel)

time: 122 us -> 119 us (0.975)
  the two profiles are of different devices: /device:TPU:1 before, /device:TPU:96 now
where the time goes in v5:
time: 119 us
  Pallas kernels  116 us (97%)
  local copies, waits for them, and re-layouts  1.59 us (1%)
  between operations  1.29 us (1%)
    pallas_call x1, Pallas kernels, shards(): pl.pallas_call(kernel, out_shape=(out, out), in_specs=[pl.BlockSpec(memor...  116 us

profile of v5, /device:TPU:96, one launch (start us, length us, event | category | flops | bytes accessed | tf_op | source)
XLA Modules:
  0.0 118.9 jit_solution(3981432766606511216)
XLA Ops:
  1.3 116.1 %shard_map.50 = (f32[4,32768]{1,0:T(4,128)S(1)}, f32[4,32768]{1,0:T(4,128)S(1)}) custom-call(f32[1]{0:T(128)S(6)} %copy.7.width_hbm, f32[4,32768]{1,0:T(4,128)} %x_ref.1, f32[4,32768]{1,0:T(4,128)} %s_ref.1), custom_call_target="tpu_custom_call" | custom-call | tf_op jit(solution)/shard_map/pallas_call | solution.py:277
  117.3 0.8 copy.8
  118.1 0.8 copy.9

commit v6 on v5

--- a/solution.py
+++ b/solution.py
@@ -207,7 +207,7 @@
     weight = jnp.sum(kern, axis=1, keepdims=True)
     block = xs[...].reshape(n, cols)
     pull = jnp.dot(kern, block, precision=HIGHEST, preferred_element_type=jnp.float32)
-    pulls[...] = ((block * weight - pull) / (n * width)).reshape(pulls.shape)
+    pulls[...] = ((block * weight - pull) / width).reshape(pulls.shape)
     each(1, GROUPS, lambda k: r_out(k).start())
     own_r = pltpu.make_async_copy(pulls.at[g], repel_ref.at[:, columns(g)], own.at[2])
     own_r.start()
@@ -219,7 +219,7 @@
     def driven(scores):
         block = scores[...].reshape(n, cols)
         drive = jnp.dot(kern, block, precision=HIGHEST, preferred_element_type=jnp.float32)
-        return (drive / n).reshape(drives.shape)
+        return drive.reshape(drives.shape)
 
     drives[...] = driven(ss)
 
@@ -284,7 +284,7 @@
         + [pltpu.SMEM((1,), jnp.float32), dma((7,))] + [dma((2,))] * 6 + [whole] * 2 + [dma((9,))],
         compiler_params=pltpu.CompilerParams(collective_id=0, has_side_effects=True, vmem_limit_bytes=55050240),
     )(kernel_width, particles, scores)
-    return (drive, repel)
+    return (drive / n, repel / n)
 
 
 def solution(mesh):

time: 119 us -> 119 us (level)
  local copies, waits for them, and re-layouts: 1.59 us -> 0 us
  other arithmetic: 0 us -> 1.24 us
    unnamed x2 -> x0, local copies, waits for them, and re-layouts: 1.59 us -> none
    div x0 -> x1, other arithmetic: none -> 1.24 us  [shards(): return (drive / n, repel / n)]
where the time goes in v6:
time: 119 us
  Pallas kernels  116 us (97%)
  between operations  1.28 us (1%)
  other arithmetic  1.24 us (1%)
    pallas_call x1, Pallas kernels, shards(): pl.pallas_call(kernel, out_shape=(out, out), in_specs=[pl.BlockSpec(memor...  116 us

profile of v6, /device:TPU:96, one launch (start us, length us, event | category | flops | bytes accessed | tf_op | source)
XLA Modules:
  0.0 118.6 jit_solution(14737984189013400987)
XLA Ops:
  1.3 116.1 %shard_map.50 = (f32[4,32768]{1,0:T(4,128)S(1)}, f32[4,32768]{1,0:T(4,128)S(1)}) custom-call(f32[1]{0:T(128)S(6)} %copy.5.width_hbm, f32[4,32768]{1,0:T(4,128)} %x_ref.1, f32[4,32768]{1,0:T(4,128)} %s_ref.1), custom_call_target="tpu_custom_call" | custom-call | tf_op jit(solution)/shard_map/pallas_call | solution.py:277
  117.3 1.2 %broadcast_multiply_fusion = (f32[4,32768]{1,0:T(4,128)}, f32[4,32768]{1,0:T(4,128)}) fusion(f32[4,32768]{1,0:T(4,128)S(1)} %get-tuple-element.5, f32[4,32768]{1,0:T(4,128)S(1)} %get-tuple-element.4), kind=kLoop, calls=%fused_computation | loop fusion | flops 262144 | bytes 2097152 | tf_op jit(solution)/shard_map/div | solution.py:287

commit v7 on v6

--- a/solution.py
+++ b/solution.py
@@ -123,6 +123,8 @@
     own_s.start()
     get_width.start()
     own_t.start()
+    each(1, Y, lambda k: to_owner(k, 0, 5))
+    each(1, Y, lambda k: to_twin(k, 3, 6))
 
     @pl.when(c != 0)
     def _():
@@ -164,8 +166,6 @@
     def _():
         each(0, Y, lambda k: to_owner(k, 3, 5))
         each(0, Y, lambda k: to_twin(k, 0, 6))
-        each(1, Y, lambda k: to_owner(k, 0, 5))
-        each(1, Y, lambda k: to_twin(k, 3, 6))
 
 
     @pl.when(c == 0)
@@ -179,8 +179,6 @@
         each(0, Y, lambda k: to_twin(k, 2, 4))
         each(0, Y, lambda k: to_owner(k, 3, 5))
         each(0, Y, lambda k: to_twin(k, 0, 6))
-        each(1, Y, lambda k: to_owner(k, 0, 5))
-        each(1, Y, lambda k: to_twin(k, 3, 6))
         await_all(lined, LINE - 1, b_sem.at[1])
         gathered[owner] = jnp.sum(lined[...], axis=0)
         each(PLANE // 2, PLANE, lambda k: gather(k).start())

time: 119 us -> 119 us (level)
  no operation moved by 1% of the time
where the time goes in v7:
time: 119 us
  Pallas kernels  116 us (97%)
  between operations  1.28 us (1%)
  other arithmetic  1.24 us (1%)
    pallas_call x1, Pallas kernels, shards(): pl.pallas_call(kernel, out_shape=(out, out), in_specs=[pl.BlockSpec(memor...  116 us

profile of v7, /device:TPU:96, one launch (start us, length us, event | category | flops | bytes accessed | tf_op | source)
XLA Modules:
  0.0 118.6 jit_solution(16309046817783073873)
XLA Ops:
  1.3 116.1 %shard_map.50 = (f32[4,32768]{1,0:T(4,128)S(1)}, f32[4,32768]{1,0:T(4,128)S(1)}) custom-call(f32[1]{0:T(128)S(6)} %copy.5.width_hbm, f32[4,32768]{1,0:T(4,128)} %x_ref.1, f32[4,32768]{1,0:T(4,128)} %s_ref.1), custom_call_target="tpu_custom_call" | custom-call | tf_op jit(solution)/shard_map/pallas_call | solution.py:275
  117.3 1.2 %broadcast_multiply_fusion = (f32[4,32768]{1,0:T(4,128)}, f32[4,32768]{1,0:T(4,128)}) fusion(f32[4,32768]{1,0:T(4,128)S(1)} %get-tuple-element.5, f32[4,32768]{1,0:T(4,128)S(1)} %get-tuple-element.4), kind=kLoop, calls=%fused_computation | loop fusion | flops 262144 | bytes 2097152 | tf_op jit(solution)/shard_map/div | solution.py:285
